TPU v7x, 256 devices: a whole 4x4x8 slice. The times are simulated.
256 devices in a mesh: fx: 8 (over y, core), fy: 8 (over z), col: 4 (over x).
Axes of the slice: x: 4, y: 4, z: 8, core: 2. Of those that a mesh axis runs over, the one named last changes fastest.
Arguments:
- x_velocity: bfloat16 [512, 512, 1024], P('fx', 'fy', 'col'), may hold values from -6 to 6
- y_velocity: bfloat16 [512, 512, 1024], P('fx', 'fy', 'col'), may hold values from -6 to 6
- z_velocity: bfloat16 [512, 512, 1024], P('fx', 'fy', 'col'), may hold values from -6 to 6
- source: bfloat16 [512, 512, 1024], P('fx', 'fy', 'col'), may hold values from -6 to 6
- coarse_adjoint: float32 [65536, 512], P(('fx', 'fy'), 'col'), may hold values from -6 to 6
- send_slot: int32 [65536], P(('fx', 'fy')), may hold values from 0 to 2047, as said below
- recv_index: int32 [65536], P(('fx', 'fy')), may hold values from 0 to 2047, as said below
Outputs:
- indicator: float32 [4, 65536], P('col', ('fx', 'fy'))
Inputs may be any that keep to these rules, and one draw needn't show every extreme that they name: `send_slot`: within each device's block of 1024 entries, each value d * 32 + s names a slot s to device d of the fx, fy plane; no slot twice; every device sends at most 32 columns to one device, and some device sends exactly 32 to some device. `recv_index`: within each device's block of 1024 entries, each value o * 32 + s names the column that device o stores with send slot (this device) * 32 + s; every device receives exactly 1024 columns, each once.
All inputs are finite; a program needn't handle non-finite values.
Results may differ from a plain program's by a relative error of at most 0.0003.
Values may be sent and summed in bfloat16 or wider, within the bound.
A program may use at most 64 MiB of HBM per device.

v0:
```python
import math

import jax
import jax.numpy as jnp
from jax import lax
from jax.sharding import PartitionSpec as P


def passed_along(value, axis, steps):
    count = lax.axis_size(axis)
    leading, last = (max(0, -steps), min(count, count - steps))
    return lax.ppermute(value, axis, [(source, source + steps) for source in range(leading, last)])


def prolong_matrix(coarse_len):
    coarse_rows = jnp.arange(coarse_len, dtype=jnp.int32)[:, None]
    fine_cols = jnp.arange(2 * coarse_len, dtype=jnp.int32)[None, :]
    centre = fine_cols // 2
    beside = jnp.clip(centre + jnp.where(fine_cols % 2 == 0, -1, 1), 0, coarse_len - 1)
    return 0.75 * (coarse_rows == centre).astype(jnp.float32) + 0.25 * (
        coarse_rows == beside
    ).astype(jnp.float32)


def per_device(x_velocity, y_velocity, z_velocity, source, coarse_adjoint, send_slot, recv_index):
    plane_first = lax.axis_size("fx")
    plane_second = lax.axis_size("fy")
    owners = plane_first * plane_second
    pencils, coarse_len = coarse_adjoint.shape
    capacity = 2 * pencils // owners
    fine_first, fine_second, fine_len = x_velocity.shape
    half_first = fine_first // 2
    half_second = fine_second // 2
    matrix = prolong_matrix(coarse_len)
    width = coarse_adjoint.shape[1]
    rows_stored = jnp.arange(pencils, dtype=jnp.int32)
    slot_source = jnp.zeros((owners * capacity,), jnp.int32).at[send_slot].set(rows_stored)
    slot_filled = jnp.zeros((owners * capacity,), jnp.bool_).at[send_slot].set(True)
    send_buffer = jnp.where(slot_filled[:, None], coarse_adjoint[slot_source], jnp.float32(0.0))
    arrived = lax.all_to_all(
        send_buffer.reshape(owners, capacity, width),
        ("fx", "fy"),
        split_axis=0,
        concat_axis=0,
        tiled=True,
    )
    placed = arrived.reshape(owners * capacity, width)[recv_index]
    first_rim = passed_along(x_velocity[0:1], "fx", -1)
    second_rim = passed_along(y_velocity[:, 0:1], "fy", -1)
    first_blocks = (
        x_velocity.reshape(half_first, 2, half_second, 2, fine_len)[:, 0]
        .astype(jnp.float32)
        .sum(axis=2)
    )
    first_edge = first_rim.reshape(1, half_second, 2, fine_len).astype(jnp.float32).sum(axis=2)
    first_part = jnp.concatenate([first_blocks[1:], first_edge], 0) - first_blocks
    second_blocks = (
        y_velocity.reshape(half_first, 2, half_second, 2, fine_len)[:, :, :, 0]
        .astype(jnp.float32)
        .sum(axis=1)
    )
    second_edge = second_rim.reshape(half_first, 2, 1, fine_len).astype(jnp.float32).sum(axis=1)
    second_part = jnp.concatenate([second_blocks[:, 1:], second_edge], 1) - second_blocks
    third_blocks = (
        z_velocity.astype(jnp.float32)
        .reshape(half_first, 2, half_second, 2, fine_len)
        .sum(axis=(1, 3))
        .reshape(pencils, fine_len)
    )
    third_edge = passed_along(third_blocks[:, 0:1], "col", -1)
    third_part = jnp.concatenate([third_blocks[:, 1:], third_edge], 1) - third_blocks
    source_blocks = (
        source.astype(jnp.float32)
        .reshape(half_first, 2, half_second, 2, fine_len)
        .sum(axis=(1, 3))
        .reshape(pencils, fine_len)
    )
    sums = (first_part + second_part).reshape(pencils, fine_len) + third_part - source_blocks
    reduced = lax.dot_general(
        sums,
        matrix,
        (((1,), (1,)), ((), ())),
        precision=lax.Precision.HIGHEST,
        preferred_element_type=jnp.float32,
    )
    values = jnp.sum(placed * reduced, axis=-1)
    values = values * (1.0 / math.sqrt(4 * fine_len))
    back_buffer = jnp.zeros((owners * capacity,), jnp.float32).at[recv_index].set(values)
    returned = lax.all_to_all(
        back_buffer.reshape(owners, capacity), ("fx", "fy"), split_axis=0, concat_axis=0, tiled=True
    )
    return returned.reshape(owners * capacity)[send_slot].reshape(1, pencils)


def solution(mesh):
    return jax.shard_map(
        per_device,
        mesh=mesh,
        in_specs=(
            P("fx", "fy", "col"),
            P("fx", "fy", "col"),
            P("fx", "fy", "col"),
            P("fx", "fy", "col"),
            P(("fx", "fy"), "col"),
            P(("fx", "fy")),
            P(("fx", "fy")),
        ),
        out_specs=P("col", ("fx", "fy")),
        check_vma=False,
    )
```

profile of v0, /device:TPU:1, one launch (start us, length us, event | category | flops | bytes accessed | tf_op | source)
XLA Modules:
  0.0 129.4 jit_solution(13263001499801496868)
XLA Ops:
  0.0 0.0 copy-start
  0.0 0.7 broadcast_clamp_fusion
  0.8 4.3 %scatter_custom_fusion.1 = s32[2048]{0:T(1024)S(1)} fusion(s32[1024]{0:T(1024)S(1)} %get-tuple-element.6, s32[1024]{0:T(1024)S(1)} %iota.13, s32[]{:T(128)} %constant.46.clone.1), kind=kCustom, calls=%fused_computation.35 | custom fusion | bytes 8196 | tf_op jit(solution)/shard_map/scatter | solution.py:37
  5.1 4.3 %scatter_custom_fusion = pred[2048]{0:T(1024)(128)(4,1)S(1)} fusion(s32[1024]{0:T(1024)S(1)} %get-tuple-element.6, pred[1024]{0:T(1024)(128)(4,1)S(1)} %broadcast.128, pred[]{:T(512)} %constant.48.clone.1), kind=kCustom, calls=%fused_computation.39 | custom fusion | bytes 2049 | tf_op jit(solution)/shard_map/scatter | solution.py:38
  9.4 0.1 broadcast_in_dim.47
  9.5 0.0 copy-done
  9.5 5.5 %gather_fusion = f32[2048,128]{1,0:T(8,128)S(1)} fusion(f32[1024,128]{1,0:T(8,128)S(1)} %copy-done, s32[2048]{0:T(1024)S(1)} %fusion.16), kind=kCustom, calls=%fused_computation | custom fusion | bytes 2105344 | tf_op jit(solution)/shard_map/gather | solution.py:39
  15.0 1.3 %broadcast_select_fusion = f32[64,32,128]{2,1,0:T(8,128)} fusion(f32[64,32,128]{2,1,0:T(8,128)S(1)} %bitcast.14, pred[64,32]{1,0:T(8,128)(4,1)S(1)} %broadcast_in_dim.47), kind=kLoop, calls=%fused_computation.19 | loop fusion | flops 262144 | bytes 2099200 | tf_op jit(solution)/shard_map/jit(_where)/select_n | solution.py:39
  16.3 13.2 %all-to-all-start = ((f32[64,32,128]{2,1,0:T(8,128)}), f32[64,32,128]{2,1,0:T(8,128)S(1)}, u32[]{:S(2)}, u32[]{:S(2)}) async-start(f32[64,32,128]{2,1,0:T(8,128)} %broadcast_select_fusion), calls=%async_computation | async-start | bytes 2097152 | tf_op jit(solution)/shard_map/all_to_all | solution.py:40
  29.5 0.8 slice.26
  30.3 2.3 %collective-permute-start = (bf16[1,64,256]{2,1,0:T(8,128)(2,1)S(1)}, bf16[1,64,256]{2,1,0:T(8,128)(2,1)S(1)}, u32[]{:S(2)}, u32[]{:S(2)}) collective-permute-start(bf16[1,64,256]{2,1,0:T(8,128)(2,1)S(1)} %slice.26), channel_id=1, source_target_pairs={{32,0},{64,32},{96,64},{128,96},{160,128},{192,160},{224,192},{33,... | collective-permute-start | bytes 98312 | tf_op jit(solution)/shard_map/ppermute | solution.py:12
  32.6 1.0 slice.29
  33.6 1.3 collective-permute-start.1
  34.9 5.1 %reshape.164 = f32[32,2,32,2,256]{4,3,2,1,0:T(2,128)} reshape(bf16[64,64,256]{2,1,0:T(8,128)(2,1)} %param.9) | data formatting | bytes 6291456 | tf_op jit(solution)/shard_map/reshape | solution.py:66
  40.0 5.5 %reduce_sum.73 = f32[32,32,256]{2,1,0:T(8,128)S(1)} reduce(f32[32,2,32,2,256]{4,3,2,1,0:T(2,128)} %reshape.164, f32[]{:T(128)} %constant.45.clone.1), dimensions={1,3}, to_apply=%region_6.7 | reduce | flops 786432 | bytes 5242884 | tf_op jit(solution)/shard_map/reduce_sum | solution.py:67
  45.5 0.8 slice.43
  46.3 1.5 %collective-permute-start.2 = (f32[1024,1]{1,0:T(8,128)}, f32[1024,1]{1,0:T(8,128)}, u32[]{:S(2)}, u32[]{:S(2)}) collective-permute-start(f32[1024,1]{1,0:T(8,128)} %slice.43), channel_id=1, source_target_pairs={{1,0},{2,1},{3,2},{5,4},{6,5},{7,6},{9,8},{10,9},{11,10},{13,12},{... | collective-permute-start | bytes 12296 | tf_op jit(solution)/shard_map/ppermute | solution.py:12
  47.8 4.1 %reshape.151 = bf16[32,2,32,2,256]{4,3,2,1,0:T(2,128)(2,1)} reshape(bf16[64,64,256]{2,1,0:T(8,128)(2,1)} %param.7) | data formatting | bytes 4194304 | tf_op jit(solution)/shard_map/reshape | solution.py:51
  51.9 0.0 copy-start.3
  51.9 4.1 %reshape.152 = bf16[32,2,32,2,256]{4,3,2,1,0:T(2,128)(2,1)} reshape(bf16[64,64,256]{2,1,0:T(8,128)(2,1)} %param.8) | data formatting | bytes 4194304 | tf_op jit(solution)/shard_map/reshape | solution.py:58
  56.0 0.0 copy-done.3
  56.1 0.0 copy-start.2
  56.1 5.1 %convert_reduce_fusion = f32[32,32,256]{2,1,0:T(8,128)} fusion(bf16[32,2,32,2,256]{4,3,2,1,0:T(2,128)(2,1)} %reshape.151), kind=kLoop, calls=%fused_computation.8 | loop fusion | flops 786432 | bytes 2097152 | tf_op jit(solution)/shard_map/reduce_sum | solution.py:53
  61.2 0.0 copy-done.2
  61.2 4.4 %fusion = f32[32,32,256]{2,1,0:T(8,128)} fusion(bf16[32,2,32,2,256]{4,3,2,1,0:T(2,128)(2,1)S(1)} %copy-done.2), kind=kLoop, calls=%fused_computation.7 | loop fusion | flops 786432 | bytes 2097152 | tf_op jit(solution)/shard_map/reduce_sum | solution.py:60
  65.6 1.4 %slice.42 = f32[1024,255]{1,0:T(8,128)} slice(f32[1024,256]{1,0:T(8,128)S(1)} %bitcast.10), slice={[0:1024], [1:256]} | slice | bytes 2088960 | tf_op jit(solution)/shard_map/slice | solution.py:71
  67.0 5.1 %reshape.166 = f32[32,2,32,2,256]{4,3,2,1,0:T(2,128)} reshape(bf16[64,64,256]{2,1,0:T(8,128)(2,1)} %param.10) | data formatting | bytes 6291456 | tf_op jit(solution)/shard_map/reshape | solution.py:74
  72.1 6.5 %reduce_sum.74 = f32[32,32,256]{2,1,0:T(8,128)} reduce(f32[32,2,32,2,256]{4,3,2,1,0:T(2,128)} %reshape.166, f32[]{:T(128)} %constant.45.clone.1), dimensions={1,3}, to_apply=%region_7.8 | reduce | flops 786432 | bytes 5242884 | tf_op jit(solution)/shard_map/reduce_sum | solution.py:75
  78.6 0.0 copy-start.1
  78.6 2.4 %slice.39 = f32[31,32,256]{2,1,0:T(8,128)} slice(f32[32,32,256]{2,1,0:T(8,128)} %convert_reduce_fusion), slice={[1:32], [0:32], [0:256]} | slice | bytes 2031616 | tf_op jit(solution)/shard_map/slice | solution.py:56
  81.0 0.0 copy-done.1
  81.0 1.1 slice.41
  82.1 0.0 collective-permute-done
  82.1 0.1 reduce_sum.68
  82.2 0.0 collective-permute-done.1
  82.2 0.2 convert_reduce_fusion.1
  82.5 0.1 reduce_sum.71
  82.6 3.7 %fusion.2 = f32[32,32,256]{2,1,0:T(8,128)} fusion(f32[32,32,256]{2,1,0:T(8,128)} %convert_reduce_fusion, f32[1,32,256]{2,1,0:T(8,128)S(1)} %bitcast.15, f32[31,32,256]{2,1,0:T(8,128)} %slice.39, f32[32,32,256]{2,1,0:T(8,128)} %fusion, f32[32,1,256]{2,1,0:T(1,128)S(1)} %reduce_sum.72, f32[32,31,256]{2,1,0:T(8,128)} %slice.41), kind=kLoop, calls=%fused_computation.12 | loop fusion | flops 1310720 | bytes 5242880 | tf_op jit(solution)/shard_map/add | solution.py:78
  86.3 0.0 all-to-all-done
  86.3 2.8 %gather_fusion.1 = f32[1024,128]{1,0:T(8,128)S(1)} fusion(f32[2048,128]{1,0:T(8,128)S(1)} %bitcast.8, s32[1024]{0:T(1024)S(1)} %get-tuple-element.7), kind=kCustom, calls=%fused_computation.1 | custom fusion | bytes 1052672 | tf_op jit(solution)/shard_map/gather | solution.py:47
  89.1 0.2 copy.10
  89.3 0.0 collective-permute-done.2
  89.3 3.4 %fusion.1 = f32[1024]{0:T(1024)S(1)} fusion(f32[1024,128]{0,1:T(8,128)S(1)} %copy.10, f32[1024,256]{1,0:T(8,128)} %bitcast.13, f32[1024,256]{1,0:T(8,128)} %bitcast.12, f32[1024,256]{1,0:T(8,128)S(1)} %bitcast.11, f32[1024,1]{1,0:T(8,128)} %collective-permute-done.2, f32[1024,255]{1,0:T(8,128)} %slice.42, s32[256]{0:T(256)S(1)} %get-tuple-element.10, ...), kind=kOutput, calls=%fused_computation.10 | convolution fusion | flops 404126720 | bytes 4724736 | tf_op jit(solution)/shard_map/dot_general | solution.py:79
  92.7 4.3 %scatter_custom_fusion.2 = f32[2048]{0:T(1024)S(1)} fusion(s32[1024]{0:T(1024)S(1)} %get-tuple-element.8, f32[1024]{0:T(1024)S(1)} %broadcast_multiply_fusion, f32[]{:T(128)} %constant.45.clone.1), kind=kCustom, calls=%fused_computation.37 | custom fusion | bytes 8196 | tf_op jit(solution)/shard_map/scatter | solution.py:88
  97.1 0.1 all_to_all.10
  97.1 20.4 %all_to_all.14 = f32[64,1,32]{2,1,0:T(1,128)S(1)} all-to-all(f32[64,1,32]{2,1,0:T(1,128)S(1)} %bitcast.16), channel_id=1, replica_groups=mesh['fx'=8,'fy'=8,'col'=4] {'fx','fy'}, dimensions={0} | all-to-all | bytes 16384 | tf_op jit(solution)/shard_map/all_to_all | solution.py:89
  117.5 0.5 broadcast.168
  118.0 0.7 reduce.11
  118.7 0.1 reshape.159
  118.8 10.5 %gather_fusion.2 = f32[1024]{0:T(1024)} fusion(f32[2048]{0:T(1024)S(1)} %reshape.159, s32[1024]{0:T(1024)S(1)} %get-tuple-element.5), kind=kCustom, calls=%fused_computation.2 | custom fusion | bytes 12288 | tf_op jit(solution)/shard_map/gather | solution.py:92
  (9 shorter events, 0.1 us)
Async XLA Ops:
  0.0 9.5 %copy-start = (f32[1024,128]{1,0:T(8,128)S(1)}, f32[1024,128]{1,0:T(8,128)}, u32[]{:S(2)}) copy-start(f32[1024,128]{1,0:T(8,128)} %param.11) | copy-start | bytes 1572868
  16.3 69.9 %all-to-all-start = ((f32[64,32,128]{2,1,0:T(8,128)}), f32[64,32,128]{2,1,0:T(8,128)S(1)}, u32[]{:S(2)}, u32[]{:S(2)}) async-start(f32[64,32,128]{2,1,0:T(8,128)} %broadcast_select_fusion), calls=%async_computation | async-start | bytes 2097152 | tf_op jit(solution)/shard_map/all_to_all | solution.py:40
  30.3 51.9 %collective-permute-start = (bf16[1,64,256]{2,1,0:T(8,128)(2,1)S(1)}, bf16[1,64,256]{2,1,0:T(8,128)(2,1)S(1)}, u32[]{:S(2)}, u32[]{:S(2)}) collective-permute-start(bf16[1,64,256]{2,1,0:T(8,128)(2,1)S(1)} %slice.26), channel_id=1, source_target_pairs={{32,0},{64,32},{96,64},{128,96},{160,128},{192,160},{224,192},{33,... | collective-permute-start | bytes 98312 | tf_op jit(solution)/shard_map/ppermute | solution.py:12
  33.6 48.6 %collective-permute-start.1 = (bf16[64,1,256]{2,1,0:T(2,128)(2,1)S(1)}, bf16[64,1,256]{2,1,0:T(2,128)(2,1)S(1)}, u32[]{:S(2)}, u32[]{:S(2)}) collective-permute-start(bf16[64,1,256]{2,1,0:T(2,128)(2,1)S(1)} %slice.29), channel_id=1, source_target_pairs={{4,0},{8,4},{12,8},{16,12},{20,16},{24,20},{28,24},{5,1},{9,5},{13... | collective-permute-start | bytes 98312 | tf_op jit(solution)/shard_map/ppermute | solution.py:12
  46.3 43.0 %collective-permute-start.2 = (f32[1024,1]{1,0:T(8,128)}, f32[1024,1]{1,0:T(8,128)}, u32[]{:S(2)}, u32[]{:S(2)}) collective-permute-start(f32[1024,1]{1,0:T(8,128)} %slice.43), channel_id=1, source_target_pairs={{1,0},{2,1},{3,2},{5,4},{6,5},{7,6},{9,8},{10,9},{11,10},{13,12},{... | collective-permute-start | bytes 12296 | tf_op jit(solution)/shard_map/ppermute | solution.py:12
  51.9 4.1 %copy-start.3 = (s32[1024]{0:T(1024)S(1)}, s32[1024]{0:T(1024)}, u32[]{:S(2)}) copy-start(s32[1024]{0:T(1024)} %param.13) | copy-start | bytes 12292
  56.1 5.1 %copy-start.2 = (bf16[32,2,32,2,256]{4,3,2,1,0:T(2,128)(2,1)S(1)}, bf16[32,2,32,2,256]{4,3,2,1,0:T(2,128)(2,1)}, u32[]{:S(2)}) copy-start(bf16[32,2,32,2,256]{4,3,2,1,0:T(2,128)(2,1)} %reshape.152) | copy-start | bytes 6291460
  78.6 2.4 %copy-start.1 = (f32[32,32,256]{2,1,0:T(8,128)S(1)}, f32[32,32,256]{2,1,0:T(8,128)}, u32[]{:S(2)}) copy-start(f32[32,32,256]{2,1,0:T(8,128)} %fusion) | copy-start | bytes 3145732
where the time goes:
time: 132 us; the launch traced here: 129 us
  local copies, waits for them, and re-layouts  58.8 us (45%)
  other arithmetic  28.3 us (21%)
  blocking collectives  20.4 us (15%)
  starting transfers between devices  18.3 us (14%)
  matrix products  3.44 us (3%)
    all_to_all x1, blocking collectives, per_device(): lax.all_to_all(back_buffer.reshape(owners, capacity), ('fx', 'fy'), split...  20.4 us
    all_to_all x1, starting transfers between devices, per_device(): lax.all_to_all(send_buffer.reshape(owners, capacity, width), ('fx', 'fy')...  13.2 us
    gather x1, local copies, waits for them, and re-layouts, per_device(): return returned.reshape(owners * capacity)[send_slot].reshape(1, pencils)  10.5 us
    reduce_sum x1, other arithmetic, per_device(): source_blocks = source.astype(jnp.float32).reshape(half_first, 2, half_se...  6.48 us
    reduce_sum x1, other arithmetic, per_device(): third_blocks = z_velocity.astype(jnp.float32).reshape(half_first, 2, half...  5.48 us
    gather x1, local copies, waits for them, and re-layouts, per_device(): coarse_adjoint[slot_source]  5.46 us
    reshape x1, local copies, waits for them, and re-layouts, per_device(): third_blocks = z_velocity.astype(jnp.float32).reshape(half_first, 2, half...  5.11 us
    reshape x1, local copies, waits for them, and re-layouts, per_device(): source_blocks = source.astype(jnp.float32).reshape(half_first, 2, half_se...  5.1 us
  transfers between devices with their start and end apart: 4, of which 0 were waited for; matrix products, arithmetic and copies ran while one was open for 42% of the time, Pallas kernels for 0%

commit v1 on v0

v1 whole, which is shorter than its diff:
```python
import functools
import math

import jax
import jax.numpy as jnp
from jax import lax
from jax.experimental import pallas as pl
from jax.experimental.pallas import tpu as pltpu
from jax.sharding import PartitionSpec as P

MESH = pl.DeviceIdType.MESH
F32 = jnp.float32
BF16 = jnp.bfloat16
I32 = jnp.int32
LIMIT = 32766.0
STEPS = 64.0


def iota(shape, axis):
    return lax.broadcasted_iota(I32, shape, axis)


def restriction(fine_len, coarse_len, shift):
    fine = iota((fine_len, coarse_len), 0) - shift
    coarse = iota((fine_len, coarse_len), 1)
    centre = lax.shift_right_arithmetic(fine, 1)
    odd = fine & 1
    beside = jnp.clip(centre + 2 * odd - 1, 0, coarse_len - 1)
    weight = jnp.where(coarse == centre, 0.75, 0.0) + jnp.where(coarse == beside, 0.25, 0.0)
    return jnp.where(fine >= 0, weight, 0.0).astype(F32)


def split(value):
    high = value.astype(BF16)
    return high, (value - high.astype(F32)).astype(BF16)


def slots_of(index_ref, chunk, table):
    slot = chunk * 256 + iota((256, 128), 0)
    hot = [
        jnp.where(index_ref[a : a + 1, :] == slot, 1.0, 0.0).astype(BF16) for a in range(8)
    ]
    both = jnp.dot(jnp.concatenate(hot, axis=1), table[...], preferred_element_type=F32)
    return both[:, :128] + both[:, 128:]


def exchange(
    n_fx,
    n_fy,
    n_col,
    x_hbm,
    y_hbm,
    z_hbm,
    s_hbm,
    adj_hbm,
    recv_hbm,
    slot_hbm,
    dots_ref,
    xb,
    yb,
    zb,
    sb,
    adjb,
    recvb,
    slotb,
    xrim,
    yrim,
    zrim,
    ysend,
    zsend,
    zc,
    xm,
    bb,
    ry,
    table,
    table2,
    adjs,
    msg,
    got,
    in_sem,
    small_sem,
    rim_send,
    rim_recv,
    send_sem,
    recv_sem,
    row_sem,
):
    fx, fy, col = lax.axis_index("fx"), lax.axis_index("fy"), lax.axis_index("col")
    me = fx * n_fy + fy
    fx_before, fy_before = lax.rem(fx + n_fx - 1, n_fx), lax.rem(fy + n_fy - 1, n_fy)
    col_before, col_after = lax.rem(col + n_col - 1, n_col), lax.rem(col + 1, n_col)

    small = [
        pltpu.make_async_copy(recv_hbm, recvb, small_sem.at[0]),
        pltpu.make_async_copy(slot_hbm, slotb, small_sem.at[1]),
        pltpu.make_async_copy(adj_hbm, adjb, small_sem.at[2]),
    ]

    def inputs(g):
        return [
            pltpu.make_async_copy(y_hbm.at[g], yb.at[g], in_sem.at[0, g]),
            pltpu.make_async_copy(z_hbm.at[g], zb.at[g], in_sem.at[1, g]),
            pltpu.make_async_copy(x_hbm.at[g, :, 0], xb.at[g], in_sem.at[2, g]),
            pltpu.make_async_copy(s_hbm.at[g], sb.at[g], in_sem.at[3, g]),
        ]

    def start_yz(g, _):
        for copy in inputs(g)[:2]:
            copy.start()
        return 0

    def start_xs(g, _):
        for copy in inputs(g)[2:]:
            copy.start()
        return 0

    lax.fori_loop(0, 8, start_yz, 0)

    barrier = pltpu.get_barrier_semaphore()

    def announce(k, _):
        pl.semaphore_signal(barrier, inc=1, device_id=(lax.rem(fx + k, n_fx), fy, col), device_id_type=MESH)
        pl.semaphore_signal(barrier, inc=1, device_id=(fx, lax.rem(fy + k, n_fy), col), device_id_type=MESH)
        return 0

    lax.fori_loop(1, 8, announce, 0)
    pl.semaphore_signal(barrier, inc=1, device_id=(fx, fy, col_before), device_id_type=MESH)
    pl.semaphore_signal(barrier, inc=1, device_id=(fx, fy, col_after), device_id_type=MESH)

    lax.fori_loop(0, 8, start_xs, 0)
    for copy in small:
        copy.start()

    below = restriction(256, 128, 0)
    third = (restriction(256, 128, 1) - below).astype(BF16)
    below = below.astype(BF16)
    first_cell = jnp.where(iota((256, 128), 0) == 0, 1.0, 0.0).astype(BF16)
    third = jnp.concatenate([third, first_cell], axis=1)
    lane64 = iota((64, 128), 1)

    zc[...] = jnp.zeros_like(zc)

    def fine_yz(g, _):
        for copy in inputs(g)[:2]:
            copy.wait()
        yy = jnp.dot(yb[g, :, 0].reshape(256, 256), below, preferred_element_type=F32) + jnp.dot(
            yb[g, :, 1].reshape(256, 256), below, preferred_element_type=F32
        )
        zz = jnp.dot(zb[g, :, 0].reshape(256, 256), third, preferred_element_type=F32) + jnp.dot(
            zb[g, :, 1].reshape(256, 256), third, preferred_element_type=F32
        )
        bb[pl.ds(pl.multiple_of(g * 256, 256), 256), :] = zz[:, :128]
        edge = zc[...]
        for ii in range(4):
            i = g * 4 + ii
            block = yy[ii * 64 : ii * 64 + 64]
            ry[pl.ds(pl.multiple_of(i * 72, 8), 64), :] = block
            ysend[i] = block[0:1]
            edge = edge + jnp.where(lane64 == i, zz[ii * 64 : ii * 64 + 64, 128:], 0.0)
        zc[...] = edge
        return 0

    lax.fori_loop(0, 8, fine_yz, 0)
    zsend[...] = zc[pl.ds(0, 32, stride=2), :] + zc[pl.ds(1, 32, stride=2), :]

    pl.semaphore_wait(barrier, 2 * 7 + 2)

    def tell_column(k, _):
        pl.semaphore_signal(row_sem, inc=1, device_id=(fx, lax.rem(fy + k, n_fy), col), device_id_type=MESH)
        return 0

    lax.fori_loop(1, 8, tell_column, 0)
    rims = [
        pltpu.make_async_remote_copy(
            src_ref=x_hbm.at[0, 0, 0],
            dst_ref=xrim,
            send_sem=rim_send.at[0],
            recv_sem=rim_recv.at[0],
            device_id=(fx_before, fy, col),
            device_id_type=MESH,
        ),
        pltpu.make_async_remote_copy(
            src_ref=ysend,
            dst_ref=yrim,
            send_sem=rim_send.at[1],
            recv_sem=rim_recv.at[1],
            device_id=(fx, fy_before, col),
            device_id_type=MESH,
        ),
        pltpu.make_async_remote_copy(
            src_ref=zsend,
            dst_ref=zrim,
            send_sem=rim_send.at[2],
            recv_sem=rim_recv.at[2],
            device_id=(fx, fy, col_before),
            device_id_type=MESH,
        ),
    ]
    for copy in rims:
        copy.start()

    def fine_xs(g, _):
        for copy in inputs(g)[2:]:
            copy.wait()
        xx = jnp.dot(xb[g].reshape(256, 256), below, preferred_element_type=F32)
        ss = jnp.dot(sb[g, :, 0].reshape(256, 256), below, preferred_element_type=F32) + jnp.dot(
            sb[g, :, 1].reshape(256, 256), below, preferred_element_type=F32
        )
        rows = pl.ds(pl.multiple_of(g * 256, 256), 256)
        xm[rows, :] = xx
        bb[rows, :] = bb[rows, :] - xx - ss
        return 0

    lax.fori_loop(0, 8, fine_xs, 0)
    for copy in small:
        copy.wait()
    for copy in rims:
        copy.wait()
    inner_x = jnp.where(fx < n_fx - 1, 1.0, 0.0)
    inner_y = jnp.where(fy < n_fy - 1, 1.0, 0.0)
    inner_z = jnp.where(col < n_col - 1, 1.0, 0.0)
    xm[2048:2112, :] = inner_x * jnp.dot(xrim[...], below, preferred_element_type=F32)
    for i in range(32):
        ry[i * 72 + 64 : i * 72 + 65, :] = inner_y * yrim[i]
    last = iota((32, 128), 1) == 127
    zlast = inner_z * zrim[...]

    def finish(g, _):
        base = pl.multiple_of(g * 256, 256)
        total = (
            bb[pl.ds(base, 128, stride=2), :]
            + bb[pl.ds(base + 1, 128, stride=2), :]
            + xm[pl.ds(base + 64, 128, stride=2), :]
            + xm[pl.ds(base + 65, 128, stride=2), :]
        )
        parts = []
        for ii in range(4):
            i = g * 4 + ii
            row = pl.multiple_of(i * 72, 8)
            part = ry[pl.ds(row + 2, 32, stride=2), :] - ry[pl.ds(row, 32, stride=2), :]
            parts.append(part + jnp.where(last, pltpu.roll(zlast, 127 - i, 1), 0.0))
        total = total + jnp.concatenate(parts, axis=0)
        high, mid = split(total)
        rows = pl.ds(pl.multiple_of(g * 128, 128), 128)
        table[rows, 0:128] = high
        table[rows, 128:256] = mid
        return 0

    lax.fori_loop(0, 8, finish, 0)
    pl.semaphore_wait(row_sem, 7)

    place = iota((8, 32, 128), 2) == iota((8, 32, 128), 1) + 32 * lax.rem(fy, 4)

    def pack(t, first):
        c = lax.rem(fx + 1 + t, n_fx)
        value = slots_of(recvb, c, table)
        largest = jnp.max(jnp.abs(value), axis=1, keepdims=True)
        level = jnp.ceil(jnp.log2(jnp.maximum(largest, 1e-33)) * STEPS) + 1.0
        code = jnp.floor(value * (jnp.exp2(level * (-1.0 / STEPS)) * LIMIT) + 0.5).astype(I32)
        code = code.reshape(8, 32, 128)
        word = lax.shift_left(code[:, 0:16], 16) | (code[:, 16:32] & 0xFFFF)
        msg[pl.ds(c * 8, 8), 0:16, :] = word
        level = jnp.where(place, level.reshape(8, 32, 1), 0.0)
        msg[pl.ds(c * 8, 8), 16:17, :] = jnp.sum(level, axis=1, keepdims=True).astype(I32)

        def send(k, _):
            to = lax.rem(fy + k, n_fy)
            pltpu.make_async_remote_copy(
                src_ref=msg.at[c * 8 + to],
                dst_ref=got.at[me],
                send_sem=send_sem,
                recv_sem=recv_sem.at[me],
                device_id=(c, to, col),
                device_id_type=MESH,
            ).start()
            return 0

        lax.fori_loop(first, 8, send, 0)

    def pack_step(t, _):
        pack(t, 0)
        return 0

    lax.fori_loop(0, 7, pack_step, 0)
    pack(7, 1)
    got[me] = msg[me]

    high, mid = split(adjb[...])
    table2[:, 0:128] = high
    table2[:, 128:256] = mid

    def place_adjoint(c, _):
        adjs[pl.ds(c * 8, 8)] = slots_of(slotb, c, table2).reshape(8, 32, 128)
        return 0

    lax.fori_loop(0, 8, place_adjoint, 0)

    diagonal = iota((2, 128, 128), 1) == iota((2, 128, 128), 2)

    def take(t, skip):
        c = lax.rem(fx + 2 * n_fx - 1 - t, n_fx)

        def arrived(k, _):
            o = c * 8 + lax.rem(fy + n_fy - k, n_fy)
            pltpu.make_async_copy(got.at[o], got.at[o], recv_sem.at[o]).wait()
            return 0

        lax.fori_loop(skip, 8, arrived, 0)
        word = got[pl.ds(c * 8, 8), 0:16, :]
        upper = lax.shift_right_arithmetic(word, 16).astype(F32)
        lower = lax.shift_right_arithmetic(lax.shift_left(word, 16), 16).astype(F32)
        columns = adjs[pl.ds(c * 8, 8)]
        product = jnp.concatenate([upper, lower], axis=1) * columns
        dot = jnp.sum(product, axis=2, keepdims=True).reshape(2, 128, 1)
        dot = jnp.sum(jnp.where(diagonal, dot, 0.0), axis=1)
        level = got[pl.ds(c * 8, 8), 16:17, :].astype(F32).reshape(2, 4, 128)
        level = jnp.sum(level, axis=1)
        dots_ref[c] = dot * (jnp.exp2(level * (1.0 / STEPS)) * (1.0 / (LIMIT * math.sqrt(4 * 256))))

    def take_step(t, _):
        take(t, 0)
        return 0

    lax.fori_loop(0, 7, take_step, 0)
    take(7, 1)
    sent = msg.at[pl.ds(0, 63)]
    pltpu.make_async_copy(sent, sent, send_sem).wait()


def pick(dots_ref, slot_ref, out_ref):
    slot = slot_ref[...]
    lane = slot & 127
    row = lax.shift_right_logical(slot, 7)
    out = jnp.zeros((8, 128), F32)
    for r in range(16):
        source = jnp.broadcast_to(dots_ref[r // 2, r % 2 : r % 2 + 1, :], (8, 128))
        out = jnp.where(row == r, jnp.take_along_axis(source, lane, axis=1), out)
    out_ref[...] = out


def per_device(x_velocity, y_velocity, z_velocity, source, coarse_adjoint, send_slot, recv_index):
    n_fx, n_fy, n_col = lax.axis_size("fx"), lax.axis_size("fy"), lax.axis_size("col")
    any_spec = pl.BlockSpec(memory_space=pl.ANY)
    vmem = pl.BlockSpec(memory_space=pltpu.VMEM)
    shape5 = (8, 4, 2, 64, 256)
    dma = pltpu.SemaphoreType.DMA
    dots = pl.pallas_call(
        functools.partial(exchange, n_fx, n_fy, n_col),
        out_shape=jax.ShapeDtypeStruct((8, 2, 128), F32),
        in_specs=[any_spec] * 7,
        out_specs=vmem,
        scratch_shapes=[
            pltpu.VMEM((8, 4, 64, 256), BF16),
            pltpu.VMEM(shape5, BF16),
            pltpu.VMEM(shape5, BF16),
            pltpu.VMEM(shape5, BF16),
            pltpu.VMEM((1024, 128), F32),
            pltpu.VMEM((8, 128), I32),
            pltpu.VMEM((8, 128), I32),
            pltpu.VMEM((64, 256), BF16),
            pltpu.VMEM((32, 1, 128), F32),
            pltpu.VMEM((32, 128), F32),
            pltpu.VMEM((32, 1, 128), F32),
            pltpu.VMEM((32, 128), F32),
            pltpu.VMEM((64, 128), F32),
            pltpu.VMEM((2112, 128), F32),
            pltpu.VMEM((2048, 128), F32),
            pltpu.VMEM((32 * 72, 128), F32),
            pltpu.VMEM((1024, 256), BF16),
            pltpu.VMEM((1024, 256), BF16),
            pltpu.VMEM((64, 32, 128), F32),
            pltpu.VMEM((64, 17, 128), I32),
            pltpu.VMEM((64, 17, 128), I32),
            dma((4, 8)),
            dma((3,)),
            dma((3,)),
            dma((3,)),
            dma,
            dma((64,)),
            pltpu.SemaphoreType.REGULAR,
        ],
        compiler_params=pltpu.CompilerParams(
            collective_id=0, has_side_effects=True, vmem_limit_bytes=56 * 1024 * 1024
        ),
    )(
        x_velocity.reshape(shape5),
        y_velocity.reshape(shape5),
        z_velocity.reshape(shape5),
        source.reshape(shape5),
        coarse_adjoint,
        recv_index.reshape(8, 128),
        send_slot.reshape(8, 128),
    )
    out = pl.pallas_call(
        pick,
        out_shape=jax.ShapeDtypeStruct((8, 128), F32),
        in_specs=[vmem, vmem],
        out_specs=vmem,
    )(dots, send_slot.reshape(8, 128))
    return out.reshape(1, 1024)


def solution(mesh):
    return jax.shard_map(
        per_device,
        mesh=mesh,
        in_specs=(
            P("fx", "fy", "col"),
            P("fx", "fy", "col"),
            P("fx", "fy", "col"),
            P("fx", "fy", "col"),
            P(("fx", "fy"), "col"),
            P(("fx", "fy")),
            P(("fx", "fy")),
        ),
        out_specs=P("col", ("fx", "fy")),
        check_vma=False,
    )
```

time: 132 us -> 31.8 us (0.24); the launches traced: 129 us -> 31.7 us
  local copies, waits for them, and re-layouts: 58.8 us -> 0 us
  Pallas kernels: 0 us -> 31.7 us
  other arithmetic: 28.3 us -> 0 us
  blocking collectives: 20.4 us -> 0 us
  starting transfers between devices: 18.3 us -> 0 us
  matrix products: 3.44 us -> 0 us
    pallas_call x0 -> x2, Pallas kernels: none -> 31.7 us  [the longest x1 30.3 us: per_device(): pl.pallas_call(functools.partial(exchange, n_fx, n_fy, n_col), out_shape=...]
    reduce_sum x6 -> x0, other arithmetic: 21.6 us -> none  [the longest x1 6.48 us: per_device(): source_blocks = source.astype(jnp.float32).reshape(half_first, 2, half_se...]
    all_to_all x1 -> x0, blocking collectives: 20.4 us -> none  [per_device(): lax.all_to_all(back_buffer.reshape(owners, capacity), ('fx', 'fy'), split...]
    gather x4 -> x0, local copies, waits for them, and re-layouts: 19 us -> none  [the longest x1 10.5 us: per_device(): return returned.reshape(owners * capacity)[send_slot].reshape(1, pencils)]
    reshape x5 -> x0, local copies, waits for them, and re-layouts: 18.5 us -> none  [the longest x1 5.11 us: per_device(): third_blocks = z_velocity.astype(jnp.float32).reshape(half_first, 2, half...]
    all_to_all x1 -> x0, starting transfers between devices: 13.2 us -> none  [per_device(): lax.all_to_all(send_buffer.reshape(owners, capacity, width), ('fx', 'fy')...]
    scatter x3 -> x0, local copies, waits for them, and re-layouts: 13 us -> none  [the longest x1 4.34 us: per_device(): jnp.zeros((owners * capacity,), jnp.bool_).at[send_slot].set(True)]
    slice x6 -> x0, local copies, waits for them, and re-layouts: 7.48 us -> none  [the longest x1 2.42 us: per_device(): first_blocks[1:]]
  transfers between devices with their start and end apart: 4 -> 0, of which waited for: 0 -> 0; matrix products, arithmetic and copies ran while one was open for 42% -> 0% of each run, Pallas kernels for 0% -> 0%
where the time goes in v1:
time: 31.8 us; the launch traced here: 31.7 us
  Pallas kernels  31.7 us (100%)
    pallas_call x1, Pallas kernels, per_device(): pl.pallas_call(functools.partial(exchange, n_fx, n_fy, n_col), out_shape=...  30.3 us
    pallas_call x1, Pallas kernels, per_device(): pl.pallas_call(pick, out_shape=jax.ShapeDtypeStruct((8, 128), F32), in_sp...  1.4 us

profile of v1, /device:TPU:1, one launch (start us, length us, event | category | flops | bytes accessed | tf_op | source)
XLA Modules:
  0.0 31.7 jit_solution(4657354875727618029)
XLA Ops:
  0.0 30.3 %shard_map.73.dots_ref = f32[8,2,128]{2,1,0:T(2,128)} custom-call(bf16[8,4,2,64,256]{4,3,2,1,0:T(8,128)(2,1)} %bitcast.7, bf16[8,4,2,64,256]{4,3,2,1,0:T(8,128)(2,1)} %bitcast.8, bf16[8,4,2,64,256]{4,3,2,1,0:T(8,128)(2,1)} %bitcast.9, bf16[8,4,2,64,256]{4,3,2,1,0:T(8,128)(2,1)} %bitcast.10, f32[1024,128]{1,0:T(8,128)} %adj_hbm.1, s32[8,128]{1,0:T(8,128)} %bitcast.13, ...), custom_call_target="tpu_custom_call" | custom-call | tf_op jit(solution)/shard_map/pallas_call | solution.py:347
  30.3 1.4 %shard_map.74 = f32[8,128]{1,0:T(8,128)} custom-call(f32[8,2,128]{2,1,0:T(2,128)} %shard_map.73.dots_ref, s32[8,128]{1,0:T(8,128)} %bitcast.12), custom_call_target="tpu_custom_call" | custom-call | tf_op jit(solution)/shard_map/pallas_call | solution.py:394

commit v2 on v1

v2 whole, which is shorter than its diff:
```python
import functools
import math

import jax
import jax.numpy as jnp
from jax import lax
from jax.experimental import pallas as pl
from jax.experimental.pallas import tpu as pltpu
from jax.sharding import PartitionSpec as P

MESH = pl.DeviceIdType.MESH
F32 = jnp.float32
BF16 = jnp.bfloat16
I32 = jnp.int32
LIMIT = 32766.0
STEPS = 64.0


def iota(shape, axis):
    return lax.broadcasted_iota(I32, shape, axis)


def restriction(fine_len, coarse_len):
    fine = iota((fine_len, coarse_len), 0)
    coarse = iota((fine_len, coarse_len), 1)
    centre = lax.shift_right_logical(fine, 1)
    beside = jnp.clip(centre + 2 * (fine & 1) - 1, 0, coarse_len - 1)
    return jnp.where(coarse == centre, 0.75, 0.0) + jnp.where(coarse == beside, 0.25, 0.0)


def split(value):
    high = value.astype(BF16)
    return high, (value - high.astype(F32)).astype(BF16)


def slots_of(index_ref, first, second, table):
    row = iota((512, 128), 0)
    fx = jnp.where(row < 256, first, second)
    slot = fx * 256 + (row & 255)
    hot = [
        jnp.where(index_ref[a : a + 1, :] == slot, 1.0, 0.0).astype(BF16) for a in range(8)
    ]
    both = jnp.dot(jnp.concatenate(hot, axis=1), table[...], preferred_element_type=F32)
    return both[:, :128] + both[:, 128:]


def exchange(
    n_fx,
    n_fy,
    n_col,
    x_hbm,
    y_hbm,
    z_hbm,
    s_hbm,
    adj_hbm,
    recv_hbm,
    slot_hbm,
    dots_ref,
    xb,
    yb,
    zb,
    sb,
    adjb,
    recvb,
    slotb,
    yrim,
    zrim,
    yfirst,
    ysend,
    zsend,
    ye,
    ze,
    xs,
    zlow,
    sums,
    restricted,
    edge_rows,
    table,
    table2,
    adjs,
    msg,
    got,
    edge_sem,
    in_sem,
    small_sem,
    rim_send,
    rim_recv,
    send_sem,
    recv_sem,
    row_sem,
):
    fx, fy, col = lax.axis_index("fx"), lax.axis_index("fy"), lax.axis_index("col")
    here = fx * n_fy + fy
    fx_before, fy_before = ((fx + n_fx - 1) & 7), ((fy + n_fy - 1) & 7)
    col_before, col_after = ((col + n_col - 1) & 3), ((col + 1) & 3)

    def remote(src, dst, send, recv, to_fx, to_fy, to_col=col):
        return pltpu.make_async_remote_copy(
            src_ref=src, dst_ref=dst, send_sem=send, recv_sem=recv, device_id=(to_fx, to_fy, to_col), device_id_type=MESH
        )

    small = [
        pltpu.make_async_copy(recv_hbm, recvb, small_sem.at[0]),
        pltpu.make_async_copy(slot_hbm, slotb, small_sem.at[1]),
        pltpu.make_async_copy(adj_hbm, adjb, small_sem.at[2]),
    ]

    edge_y = pltpu.make_async_copy(y_hbm.at[:, :, :, 0:16], yb.at[:, :, :, 0:16], edge_sem.at[0])
    edge_z = pltpu.make_async_copy(z_hbm.at[:, :, :, :, 0:128], zb.at[0], edge_sem.at[1])

    def input_x(g):
        return pltpu.make_async_copy(x_hbm.at[g, :, 0], xb.at[pl.ds(8 * g, 8)], in_sem.at[2, g])

    def inputs(g):
        return [
            pltpu.make_async_copy(y_hbm.at[g, :, :, 16:64], yb.at[g, :, :, 16:64], in_sem.at[0, g]),
            pltpu.make_async_copy(z_hbm.at[g, :, :, :, 128:256], zb.at[1, g], in_sem.at[1, g]),
            pltpu.make_async_copy(s_hbm.at[g], sb.at[g], in_sem.at[3, g]),
        ]


    barrier = pltpu.get_barrier_semaphore()

    def announce(k, _):
        pl.semaphore_signal(barrier, inc=1, device_id=(fx, ((fy + k) & 7), col), device_id_type=MESH)
        pl.semaphore_signal(barrier, inc=1, device_id=(((fx + k) & 7), fy, col), device_id_type=MESH)
        return 0

    for k in range(1, 8):
        announce(k, 0)
    pl.semaphore_signal(barrier, inc=1, device_id=(fx, fy, col_before), device_id_type=MESH)
    pl.semaphore_signal(barrier, inc=1, device_id=(fx, fy, col_after), device_id_type=MESH)

    edge_y.start()
    edge_z.start()
    input_x(0).start()
    for g in range(4):
        if g < 3:
            input_x(g + 1).start()
        for copy in inputs(g):
            copy.start()
    for copy in small:
        copy.start()

    def tell_column(k, _):
        pl.semaphore_signal(row_sem, inc=1, device_id=(fx, ((fy + k) & 7), col), device_id_type=MESH)
        return 0

    rim_x = remote(x_hbm.at[0, 0, 0], xb.at[32], rim_send.at[0], rim_recv.at[0], fx_before, fy)
    rim_y = remote(ysend, yrim, rim_send.at[1], rim_recv.at[1], fx, fy_before)
    rim_z = remote(zsend, zrim, rim_send.at[2], rim_recv.at[2], fx, fy, col_before)

    def pair(t):
        return ((fx + 1 + 2 * t) & 7), ((fx + 2 + 2 * t) & 7)

    place = iota((8, 32, 128), 2) == iota((8, 32, 128), 1) + 32 * (fy & 3)

    def encode(value, first, second):
        largest = jnp.max(jnp.abs(value), axis=1, keepdims=True)
        level = jnp.ceil(jnp.log2(jnp.maximum(largest, 1e-33)) * STEPS) + 1.0
        code = jnp.floor(value * (jnp.exp2(level * (-1.0 / STEPS)) * LIMIT) + 0.5).astype(I32)
        code = code.reshape(16, 32, 128)
        word = lax.shift_left(code[:, 0:16], 16) | (code[:, 16:32] & 0xFFFF)
        level = level.reshape(16, 32, 1)
        for u, f in enumerate((first, second)):
            msg[pl.ds(f * 8, 8), 0:16, :] = word[u * 8 : u * 8 + 8]
            row = jnp.sum(jnp.where(place, level[u * 8 : u * 8 + 8], 0.0), axis=1, keepdims=True)
            msg[pl.ds(f * 8, 8), 16:17, :] = row.astype(I32)

    def send_rows(t, first, second):
        def one(f, k):
            to = (fy + k) & 7
            remote(msg.at[f * 8 + to], got.at[here], send_sem, recv_sem.at[here], f, to).start()

        for k in range(8):
            one(first, k)
        pl.when(t < 3)(lambda: one(second, 0))
        for k in range(1, 8):
            one(second, k)

    def wait_rows(f, own):
        def one(k):
            o = f * 8 + ((fy + k) & 7)
            pltpu.make_async_copy(got.at[o], got.at[o], recv_sem.at[o]).wait()

        if own is None:
            one(0)
        else:
            pl.when(jnp.logical_not(own))(lambda: one(0))
        for k in range(1, 8):
            one(k)

    def dots_of(f, columns):
        word = got[pl.ds(f * 8, 8), 0:16, :]
        upper = lax.shift_right_arithmetic(word, 16).astype(F32)
        lower = lax.shift_right_arithmetic(lax.shift_left(word, 16), 16).astype(F32)
        product = jnp.concatenate([upper, lower], axis=1) * columns
        return jnp.sum(product, axis=2, keepdims=True), got[pl.ds(f * 8, 8), 16:17, :].astype(F32)

    pl.semaphore_wait(barrier, 2 * 7 + 2)
    for k in range(1, 8):
        tell_column(k, 0)
    rim_x.start()

    below = restriction(256, 128).astype(BF16)
    below2 = jnp.concatenate([below, below], axis=0)

    lane = iota((32, 128), 1)
    halves = [slice(0, 128), slice(128, 256)]
    ye[...] = jnp.zeros_like(ye)
    edge_y.wait()
    for i in range(32):
        rows = yb[i // 8, i % 8, :, 0:16, :].astype(F32)
        yfirst[i : i + 1, :] = rows[0, 0:1] + rows[1, 0:1]
    high, mid = split(yfirst[...])
    ysend[...] = jnp.dot(jnp.concatenate([high, mid], axis=1), below2, preferred_element_type=F32)
    rim_y.start()
    edge_z.wait()
    zsend[...] = jnp.zeros_like(zsend)

    def fine_z(g, _):
        for ii in range(8):
            ze[ii, 0] = zb[0, g, ii, 0].astype(F32) + zb[0, g, ii, 1].astype(F32)
        edge = zsend[...]
        for ii in range(8):
            z = ze[ii, 0, pl.ds(0, 32, stride=2), :] + ze[ii, 0, pl.ds(1, 32, stride=2), :]
            edge = jnp.where(lane == g * 8 + ii, z[:, 0:1], edge)
            zlow[g * 8 + ii] = z
        zsend[...] = edge
        return 0

    for g in range(4):
        fine_z(g, 0)
    rim_z.start()


    def fine(g, _):
        if g == 0:
            input_x(0).wait()
        if g < 3:
            input_x(g + 1).wait()
        for copy in inputs(g):
            copy.wait()
        if g == 3:
            rim_x.wait()
            xb[32] = jnp.where(fx < n_fx - 1, xb[32], jnp.zeros_like(xb[32]))

        for ii in range(8):
            i = g * 8 + ii
            for h in range(2):
                ye[ii, h, 0:64] = yb[g, ii, 0, :, halves[h]].astype(F32) + yb[g, ii, 1, :, halves[h]].astype(F32)
                lower = xb[i, :, halves[h]].astype(F32) + sb[g, ii, 0, :, halves[h]].astype(F32)
                upper = xb[i + 1, :, halves[h]].astype(F32) - sb[g, ii, 1, :, halves[h]].astype(F32)
                xs[ii, h] = upper - lower
            ze[ii, 1] = zb[1, g, ii, 0].astype(F32) + zb[1, g, ii, 1].astype(F32)
        for ii in range(8):
            i = g * 8 + ii
            z0 = zlow[i]
            z1 = ze[ii, 1, pl.ds(0, 32, stride=2), :] + ze[ii, 1, pl.ds(1, 32, stride=2), :]
            next0, next1 = pltpu.roll(z0, 127, 1), pltpu.roll(z1, 127, 1)
            next0 = jnp.where(lane == 127, next1, next0)
            next1 = jnp.where(lane == 127, 0.0, next1)
            rows = pl.ds(g * 256 + ii * 32, 32)
            for h, change in enumerate((next0 - z0, next1 - z1)):
                rise = ye[ii, h, pl.ds(2, 32, stride=2), :] - ye[ii, h, pl.ds(0, 32, stride=2), :]
                rest = xs[ii, h, pl.ds(0, 32, stride=2), :] + xs[ii, h, pl.ds(1, 32, stride=2), :]
                high, mid = split(change + rise + rest)
                sums[rows, h * 128 : h * 128 + 128] = high
                sums[rows, 256 + h * 128 : 256 + h * 128 + 128] = mid
        rows = pl.ds(g * 256, 256)
        restricted[rows, :] = jnp.dot(sums[rows, :], below2, preferred_element_type=F32)
        return 0

    for g in range(4):
        fine(g, 0)
    small[0].wait()
    rim_y.wait()
    rim_z.wait()
    inner_y = jnp.where(fy < n_fy - 1, 1.0, 0.0)
    inner_z = jnp.where(col < n_col - 1, 1.0, 0.0)
    edge_rows[...] = inner_y * yrim[...]
    zlast = inner_z * zrim[...]
    bottom = iota((8, 128), 0) == 7

    def finish(g, _):
        for ii in range(8):
            i = g * 8 + ii
            rows = pl.ds(g * 256 + ii * 32, 32)
            total = restricted[rows, :] + jnp.where(lane == 127, pltpu.roll(zlast, 127 - i, 1), 0.0)
            row = jnp.where(bottom, edge_rows[pl.ds(i, 1), :], 0.0)
            total = jnp.concatenate([total[:24], total[24:] + row], axis=0)
            high, mid = split(total)
            table[rows, 0:128] = high
            table[rows, 128:256] = mid
        return 0

    for g in range(4):
        finish(g, 0)

    def send_residuals(t, _):
        first, second = pair(t)
        encode(slots_of(recvb, first, second, table), first, second)

        @pl.when(t == 0)
        def _():
            pl.semaphore_wait(row_sem, 7)

        send_rows(t, first, second)
        return 0

    lax.fori_loop(0, 4, send_residuals, 0)
    got[here] = msg[here]

    small[1].wait()
    small[2].wait()
    high, mid = split(adjb[...])
    table2[:, 0:128] = high
    table2[:, 128:256] = mid
    def place_columns(t, _):
        first, second = ((fx + 15 - 2 * t) & 7), ((fx + 14 - 2 * t) & 7)
        adjs[t] = slots_of(slotb, first, second, table2).reshape(2, 8, 32, 128)
        return 0

    lax.fori_loop(0, 4, place_columns, 0)
    diagonal = iota((2, 128, 128), 1) == iota((2, 128, 128), 2)
    norm = 1.0 / (LIMIT * math.sqrt(4 * 256))

    def take_rows(t, _):
        for u, f in enumerate((((fx + 15 - 2 * t) & 7), ((fx + 14 - 2 * t) & 7))):
            wait_rows(f, t == 3 if u == 1 else None)
            dot, level = dots_of(f, adjs[t, u])
            dot = jnp.sum(jnp.where(diagonal, dot.reshape(2, 128, 1), 0.0), axis=1)
            level = jnp.sum(level.reshape(2, 4, 128), axis=1)
            dots_ref[f] = dot * (jnp.exp2(level * (1.0 / STEPS)) * norm)
        return 0

    lax.fori_loop(0, 4, take_rows, 0)

    sent = msg.at[pl.ds(0, 63)]
    pltpu.make_async_copy(sent, sent, send_sem).wait()


def pick(dots_ref, slot_ref, out_ref):
    slot = slot_ref[...]
    lane = slot & 127
    row = lax.shift_right_logical(slot, 7)
    out = jnp.zeros((8, 128), F32)
    for r in range(16):
        source = jnp.broadcast_to(dots_ref[r // 2, r % 2 : r % 2 + 1, :], (8, 128))
        out = jnp.where(row == r, jnp.take_along_axis(source, lane, axis=1), out)
    out_ref[...] = out


def per_device(x_velocity, y_velocity, z_velocity, source, coarse_adjoint, send_slot, recv_index):
    n_fx, n_fy, n_col = lax.axis_size("fx"), lax.axis_size("fy"), lax.axis_size("col")
    any_spec = pl.BlockSpec(memory_space=pl.ANY)
    vmem = pl.BlockSpec(memory_space=pltpu.VMEM)
    shape5 = (4, 8, 2, 64, 256)
    dma = pltpu.SemaphoreType.DMA
    dots = pl.pallas_call(
        functools.partial(exchange, n_fx, n_fy, n_col),
        out_shape=jax.ShapeDtypeStruct((8, 2, 128), F32),
        in_specs=[any_spec] * 7,
        out_specs=vmem,
        scratch_shapes=[
            pltpu.VMEM((33, 64, 256), BF16),
            pltpu.VMEM(shape5, BF16),
            pltpu.VMEM((2, 4, 8, 2, 64, 128), BF16),
            pltpu.VMEM(shape5, BF16),
            pltpu.VMEM((1024, 128), F32),
            pltpu.VMEM((8, 128), I32),
            pltpu.VMEM((8, 128), I32),
            pltpu.VMEM((32, 128), F32),
            pltpu.VMEM((32, 128), F32),
            pltpu.VMEM((32, 256), F32),
            pltpu.VMEM((32, 128), F32),
            pltpu.VMEM((32, 128), F32),
            pltpu.VMEM((8, 2, 72, 128), F32),
            pltpu.VMEM((8, 2, 64, 128), F32),
            pltpu.VMEM((8, 2, 64, 128), F32),
            pltpu.VMEM((32, 32, 128), F32),
            pltpu.VMEM((1024, 512), BF16),
            pltpu.VMEM((1024, 128), F32),
            pltpu.VMEM((32, 128), F32),
            pltpu.VMEM((1024, 256), BF16),
            pltpu.VMEM((1024, 256), BF16),
            pltpu.VMEM((4, 2, 8, 32, 128), F32),
            pltpu.VMEM((64, 17, 128), I32),
            pltpu.VMEM((64, 17, 128), I32),
            dma((2,)),
            dma((4, 4)),
            dma((3,)),
            dma((3,)),
            dma((3,)),
            dma,
            dma((64,)),
            pltpu.SemaphoreType.REGULAR,
        ],
        compiler_params=pltpu.CompilerParams(
            collective_id=0, has_side_effects=True, vmem_limit_bytes=56 * 1024 * 1024
        ),
    )(
        x_velocity.reshape(shape5),
        y_velocity.reshape(shape5),
        z_velocity.reshape(shape5),
        source.reshape(shape5),
        coarse_adjoint,
        recv_index.reshape(8, 128),
        send_slot.reshape(8, 128),
    )
    out = pl.pallas_call(
        pick,
        out_shape=jax.ShapeDtypeStruct((8, 128), F32),
        in_specs=[vmem, vmem],
        out_specs=vmem,
    )(dots, send_slot.reshape(8, 128))
    return out.reshape(1, 1024)


def solution(mesh):
    return jax.shard_map(
        per_device,
        mesh=mesh,
        in_specs=(
            P("fx", "fy", "col"),
            P("fx", "fy", "col"),
            P("fx", "fy", "col"),
            P("fx", "fy", "col"),
            P(("fx", "fy"), "col"),
            P(("fx", "fy")),
            P(("fx", "fy")),
        ),
        out_specs=P("col", ("fx", "fy")),
        check_vma=False,
    )
```

time: 31.8 us -> 30.2 us (0.950)
  Pallas kernels: 31.7 us -> 30 us
    pallas_call x1, Pallas kernels: 30.3 us -> 28.6 us  [per_device(): pl.pallas_call(functools.partial(exchange, n_fx, n_fy, n_col), out_shape=...]
where the time goes in v2:
time: 30.2 us; the launch traced here: 30 us
  Pallas kernels  30 us (99%)
    pallas_call x1, Pallas kernels, per_device(): pl.pallas_call(functools.partial(exchange, n_fx, n_fy, n_col), out_shape=...  28.6 us
    pallas_call x1, Pallas kernels, per_device(): pl.pallas_call(pick, out_shape=jax.ShapeDtypeStruct((8, 128), F32), in_sp...  1.4 us

profile of v2, /device:TPU:1, one launch (start us, length us, event | category | flops | bytes accessed | tf_op | source)
XLA Modules:
  0.0 30.0 jit_solution(11802278772916665357)
XLA Ops:
  0.0 28.6 %shard_map.73.dots_ref = f32[8,2,128]{2,1,0:T(2,128)} custom-call(bf16[4,8,2,64,256]{4,3,2,1,0:T(8,128)(2,1)} %bitcast.7, bf16[4,8,2,64,256]{4,3,2,1,0:T(8,128)(2,1)} %bitcast.8, bf16[4,8,2,64,256]{4,3,2,1,0:T(8,128)(2,1)} %bitcast.9, bf16[4,8,2,64,256]{4,3,2,1,0:T(8,128)(2,1)} %bitcast.10, f32[1024,128]{1,0:T(8,128)} %adj_hbm.1, s32[8,128]{1,0:T(8,128)} %bitcast.13, ...), custom_call_target="tpu_custom_call" | custom-call | tf_op jit(solution)/shard_map/pallas_call | solution.py:360
  28.6 1.4 %shard_map.74 = f32[8,128]{1,0:T(8,128)} custom-call(f32[8,2,128]{2,1,0:T(2,128)} %shard_map.73.dots_ref, s32[8,128]{1,0:T(8,128)} %bitcast.12), custom_call_target="tpu_custom_call" | custom-call | tf_op jit(solution)/shard_map/pallas_call | solution.py:411

commit v3 on v2

--- a/solution.py
+++ b/solution.py
@@ -359,7 +359,7 @@
     dma = pltpu.SemaphoreType.DMA
     dots = pl.pallas_call(
         functools.partial(exchange, n_fx, n_fy, n_col),
-        out_shape=jax.ShapeDtypeStruct((8, 2, 128), F32),
+        out_shape=pltpu.VMEM((8, 2, 128), F32),
         in_specs=[any_spec] * 7,
         out_specs=vmem,
         scratch_shapes=[
@@ -397,7 +397,7 @@
             pltpu.SemaphoreType.REGULAR,
         ],
         compiler_params=pltpu.CompilerParams(
-            collective_id=0, has_side_effects=True, vmem_limit_bytes=56 * 1024 * 1024
+            collective_id=0, has_side_effects=True, vmem_limit_bytes=58720256
         ),
     )(
         x_velocity.reshape(shape5),
@@ -413,6 +413,7 @@
         out_shape=jax.ShapeDtypeStruct((8, 128), F32),
         in_specs=[vmem, vmem],
         out_specs=vmem,
+        compiler_params=pltpu.CompilerParams(vmem_limit_bytes=1024 * 1024),
     )(dots, send_slot.reshape(8, 128))
     return out.reshape(1, 1024)
 

time: 30.2 us -> 28.8 us (0.954)
  Pallas kernels: 30 us -> 28.7 us
    pallas_call x1, Pallas kernels: 1.4 us -> 0.68 us  [per_device(): pl.pallas_call(pick, out_shape=jax.ShapeDtypeStruct((8, 128), F32), in_sp...]
    pallas_call x1, Pallas kernels: 28.6 us -> 28 us  [per_device(): pl.pallas_call(functools.partial(exchange, n_fx, n_fy, n_col), out_shape=...]
where the time goes in v3:
time: 28.8 us; the launch traced here: 28.7 us
  Pallas kernels  28.7 us (100%)
    pallas_call x1, Pallas kernels, per_device(): pl.pallas_call(functools.partial(exchange, n_fx, n_fy, n_col), out_shape=...  28 us
    pallas_call x1, Pallas kernels, per_device(): pl.pallas_call(pick, out_shape=jax.ShapeDtypeStruct((8, 128), F32), in_sp...  0.68 us

profile of v3, /device:TPU:1, one launch (start us, length us, event | category | flops | bytes accessed | tf_op | source)
XLA Modules:
  0.0 28.7 jit_solution(8397369982002988742)
XLA Ops:
  0.0 0.0 copy-start
  0.0 28.0 %shard_map.73.dots_ref = f32[8,2,128]{2,1,0:T(2,128)S(1)} custom-call(bf16[4,8,2,64,256]{4,3,2,1,0:T(8,128)(2,1)} %bitcast.9, bf16[4,8,2,64,256]{4,3,2,1,0:T(8,128)(2,1)} %bitcast.10, bf16[4,8,2,64,256]{4,3,2,1,0:T(8,128)(2,1)} %bitcast.11, bf16[4,8,2,64,256]{4,3,2,1,0:T(8,128)(2,1)} %bitcast.12, f32[1024,128]{1,0:T(8,128)} %adj_hbm.1, s32[8,128]{1,0:T(8,128)} %bitcast.13, ...), custom_call_target="tpu_custom_call" | custom-call | tf_op jit(solution)/shard_map/pallas_call | solution.py:360
  28.0 0.0 copy-done
  28.0 0.7 %shard_map.74 = f32[8,128]{1,0:T(8,128)} custom-call(f32[8,2,128]{2,1,0:T(2,128)S(1)} %shard_map.73.dots_ref, s32[8,128]{1,0:T(8,128)S(1)} %bitcast.8), custom_call_target="tpu_custom_call" | custom-call | tf_op jit(solution)/shard_map/pallas_call | solution.py:411
Async XLA Ops:
  0.0 28.0 %copy-start = (s32[1024]{0:T(1024)S(1)}, s32[1024]{0:T(1024)}, u32[]{:S(2)}) copy-start(s32[1024]{0:T(1024)} %param.12) | copy-start | bytes 12292

commit v4 on v3

--- a/solution.py
+++ b/solution.py
@@ -34,8 +34,8 @@
 
 
 def slots_of(index_ref, first, second, table):
-    row = iota((512, 128), 0)
-    fx = jnp.where(row < 256, first, second)
+    row = iota((256 if second is None else 512, 128), 0)
+    fx = first if second is None else jnp.where(row < 256, first, second)
     slot = fx * 256 + (row & 255)
     hot = [
         jnp.where(index_ref[a : a + 1, :] == slot, 1.0, 0.0).astype(BF16) for a in range(8)
@@ -159,24 +159,24 @@
         largest = jnp.max(jnp.abs(value), axis=1, keepdims=True)
         level = jnp.ceil(jnp.log2(jnp.maximum(largest, 1e-33)) * STEPS) + 1.0
         code = jnp.floor(value * (jnp.exp2(level * (-1.0 / STEPS)) * LIMIT) + 0.5).astype(I32)
-        code = code.reshape(16, 32, 128)
+        code = code.reshape(-1, 32, 128)
         word = lax.shift_left(code[:, 0:16], 16) | (code[:, 16:32] & 0xFFFF)
-        level = level.reshape(16, 32, 1)
-        for u, f in enumerate((first, second)):
+        level = level.reshape(-1, 32, 1)
+        for u, f in enumerate((first,) if second is None else (first, second)):
             msg[pl.ds(f * 8, 8), 0:16, :] = word[u * 8 : u * 8 + 8]
             row = jnp.sum(jnp.where(place, level[u * 8 : u * 8 + 8], 0.0), axis=1, keepdims=True)
             msg[pl.ds(f * 8, 8), 16:17, :] = row.astype(I32)
 
+    def send_row(f, k):
+        to = (fy + k) & 7
+        remote(msg.at[f * 8 + to], got.at[here], send_sem, recv_sem.at[here], f, to).start()
+
     def send_rows(t, first, second):
-        def one(f, k):
-            to = (fy + k) & 7
-            remote(msg.at[f * 8 + to], got.at[here], send_sem, recv_sem.at[here], f, to).start()
-
         for k in range(8):
-            one(first, k)
-        pl.when(t < 3)(lambda: one(second, 0))
+            send_row(first, k)
+        pl.when(t < 3)(lambda: send_row(second, 0))
         for k in range(1, 8):
-            one(second, k)
+            send_row(second, k)
 
     def wait_rows(f, own):
         def one(k):
@@ -300,15 +300,16 @@
     def send_residuals(t, _):
         first, second = pair(t)
         encode(slots_of(recvb, first, second, table), first, second)
-
-        @pl.when(t == 0)
-        def _():
+        send_rows(t, first, second)
+        return 0
+
+    for u, f in enumerate(pair(0)):
+        encode(slots_of(recvb, f, None, table), f, None)
+        if u == 0:
             pl.semaphore_wait(row_sem, 7)
-
-        send_rows(t, first, second)
-        return 0
-
-    lax.fori_loop(0, 4, send_residuals, 0)
+        for k in range(8):
+            send_row(f, k)
+    lax.fori_loop(1, 4, send_residuals, 0)
     got[here] = msg[here]
 
     small[1].wait()

time: 28.8 us -> 28.7 us (level)
  no operation moved by 1% of the time
where the time goes in v4:
time: 28.7 us; the launch traced here: 28.6 us
  Pallas kernels  28.6 us (100%)
    pallas_call x1, Pallas kernels, per_device(): pl.pallas_call(functools.partial(exchange, n_fx, n_fy, n_col), out_shape=...  27.9 us
    pallas_call x1, Pallas kernels, per_device(): pl.pallas_call(pick, out_shape=jax.ShapeDtypeStruct((8, 128), F32), in_sp...  0.68 us

profile of v4, /device:TPU:1, one launch (start us, length us, event | category | flops | bytes accessed | tf_op | source)
XLA Modules:
  0.0 28.6 jit_solution(95831825327406150)
XLA Ops:
  0.0 0.0 copy-start
  0.0 27.9 %shard_map.73.dots_ref = f32[8,2,128]{2,1,0:T(2,128)S(1)} custom-call(bf16[4,8,2,64,256]{4,3,2,1,0:T(8,128)(2,1)} %bitcast.9, bf16[4,8,2,64,256]{4,3,2,1,0:T(8,128)(2,1)} %bitcast.10, bf16[4,8,2,64,256]{4,3,2,1,0:T(8,128)(2,1)} %bitcast.11, bf16[4,8,2,64,256]{4,3,2,1,0:T(8,128)(2,1)} %bitcast.12, f32[1024,128]{1,0:T(8,128)} %adj_hbm.1, s32[8,128]{1,0:T(8,128)} %bitcast.13, ...), custom_call_target="tpu_custom_call" | custom-call | tf_op jit(solution)/shard_map/pallas_call | solution.py:361
  28.0 0.0 copy-done
  28.0 0.7 %shard_map.74 = f32[8,128]{1,0:T(8,128)} custom-call(f32[8,2,128]{2,1,0:T(2,128)S(1)} %shard_map.73.dots_ref, s32[8,128]{1,0:T(8,128)S(1)} %bitcast.8), custom_call_target="tpu_custom_call" | custom-call | tf_op jit(solution)/shard_map/pallas_call | solution.py:412
Async XLA Ops:
  0.0 28.0 %copy-start = (s32[1024]{0:T(1024)S(1)}, s32[1024]{0:T(1024)}, u32[]{:S(2)}) copy-start(s32[1024]{0:T(1024)} %param.12) | copy-start | bytes 12292
